TPU v7x, 128 devices: a whole 4x4x4 slice. The times are simulated.
128 devices in a mesh: ctx: 64 (over x_hi, y, z, core), head: 2 (over x_lo).
Axes of the slice: x: 4 (x_hi: 2, x_lo: 2; x = x_hi * 2 + x_lo), y: 4, z: 4, core: 2. Of those that a mesh axis runs over, the one named last changes fastest.
Arguments:
- queries: bfloat16 [2, 10240, 2048], P(None, 'ctx', 'head'), may hold values from -8 to 100
- keys: bfloat16 [2, 10240, 512], P(None, 'ctx', 'head'), may hold values from -8 to 8
- values: bfloat16 [2, 10240, 512], P(None, 'ctx', 'head'), may hold values from -6 to 6
- doc_start: int32 [10240], P('ctx'), may hold values from 0 to 8320, as said below
- out_weight: bfloat16 [2, 2048, 4096], P(None, None, 'head'), may hold values from -0.25 to 0.25
Outputs:
- attended: bfloat16 [2, 10240, 4096], P(None, 'ctx', 'head')
Inputs may be any that keep to these rules, and one draw needn't show every extreme that they name: doc_start[i] is the position of the first token of the document holding row i's token; the 4 documents lie one after another from position 0, so doc_start[i] <= pos[i]; the last document starts at position (3) * 2560 + 10240 // 16.
All inputs are finite; a program needn't handle non-finite values.
Results may differ from a plain program's by a relative error of at most 0.012.
The roundings to bfloat16 on the way count: a program that leaves them out, or rounds other values in their place, can miss the bound.
Values may be sent and summed in bfloat16 or wider, within the bound.
A program may use at most 128 MiB of HBM per device.

v0:
```python
import jax
import jax.numpy as jnp
import numpy as np
from jax import lax
from jax.sharding import PartitionSpec as P

HD = 128


def rotate_pairs(tensor, positions, head_width):
    half_width = head_width // 2
    inverse_freq = jnp.asarray(
        np.power(500000.0, -np.arange(half_width) * 2.0 / head_width).astype(np.float32)
    )
    angles = positions.astype(jnp.float32)[:, None] * inverse_freq[None, :]
    cosine = jnp.cos(angles)[None, :, None, :]
    sine_part = jnp.sin(angles)[None, :, None, :]
    models, length, total_width = tensor.shape
    split_view = tensor.astype(jnp.float32).reshape(
        models, length, total_width // head_width, 2, half_width
    )
    first_half = split_view[:, :, :, 0, :]
    second_half = split_view[:, :, :, 1, :]
    turned = jnp.stack(
        [
            first_half * cosine - second_half * sine_part,
            second_half * cosine + first_half * sine_part,
        ],
        axis=3,
    )
    return turned.reshape(models, length, total_width).astype(jnp.bfloat16)


def widest_divisor(total, limit):
    for candidate in range(min(total, limit), 0, -1):
        if total % candidate == 0:
            return candidate
    return 1


def attend_block(
    state, queries_rot, key_block, value_block, query_pos, key_pos, doc_first, head_width
):
    running_max, running_sum, accumulated = state
    models, length, query_width = queries_rot.shape
    key_len = key_block.shape[1]
    kv_heads = key_block.shape[2] // head_width
    group_size = query_width // head_width // kv_heads
    query_view = queries_rot.reshape(models, length, kv_heads, group_size, head_width)
    key_view = key_block.reshape(models, key_len, kv_heads, head_width)
    value_view = value_block.reshape(models, key_len, kv_heads, head_width)
    scores = jnp.einsum(
        "mtgrd,mkgd->mgrtk", query_view, key_view, preferred_element_type=jnp.float32
    ) * head_width ** (-0.5)
    allowed = (key_pos[:, None, :] <= query_pos[None, :, None]) & (
        key_pos[:, None, :] >= doc_first[None, :, None]
    )
    allowed = allowed[:, None, None, :, :]
    block_max = jnp.max(jnp.where(allowed, scores, -1e30), axis=-1)
    new_max = jnp.maximum(running_max, block_max)
    weights = jnp.where(allowed, jnp.exp(scores - new_max[..., None]), 0.0)
    rescale = jnp.exp(running_max - new_max)
    running_sum = running_sum * rescale + jnp.sum(weights, axis=-1)
    update = jnp.einsum(
        "mgrtk,mkgd->mgrtd",
        weights.astype(jnp.bfloat16),
        value_view,
        preferred_element_type=jnp.float32,
    )
    accumulated = accumulated * rescale[..., None] + update
    return (new_max, running_sum, accumulated)


def local(queries, keys, values, doc_start, out_weight):
    cycle_size = lax.axis_size("ctx")
    own_index = lax.axis_index("ctx")
    models, length, query_width = queries.shape
    local_rows = jnp.arange(length, dtype=jnp.int32)
    query_pos = local_rows * cycle_size + own_index
    queries_rot = rotate_pairs(queries, query_pos, HD)
    keys_rot = rotate_pairs(keys, query_pos, HD)
    kv_heads = keys.shape[2] // HD
    group_size = query_width // HD // kv_heads

    def absorb_range(state, key_piece, value_piece, start_row, query_part):
        piece_len = key_piece.shape[1]
        span = widest_divisor(piece_len, 640)

        def one_span(span_index, inner_state):
            offset = span_index * span
            key_block = lax.dynamic_slice_in_dim(key_piece, offset, span, 1)
            value_block = lax.dynamic_slice_in_dim(value_piece, offset, span, 1)
            index_all = start_row + offset + jnp.arange(span, dtype=jnp.int32)
            key_pos = index_all % length * cycle_size + index_all // length
            key_pos = jnp.broadcast_to(key_pos[None, :], (key_piece.shape[0], span))
            return attend_block(
                inner_state, query_part, key_block, value_block, query_pos, key_pos, doc_start, HD
            )

        if piece_len == span:
            return one_span(0, state)
        return lax.fori_loop(0, piece_len // span, one_span, state)

    state = absorb_range(
        (
            jnp.full((models, kv_heads, group_size, length), -1e30, jnp.float32),
            jnp.zeros((models, kv_heads, group_size, length), jnp.float32),
            jnp.zeros((models, kv_heads, group_size, length, HD), jnp.float32),
        ),
        lax.all_gather(keys_rot, "ctx", axis=1, tiled=True),
        lax.all_gather(values, "ctx", axis=1, tiled=True),
        jnp.int32(0),
        queries_rot,
    )
    running_max, running_sum, accumulated = state
    context = accumulated / running_sum[..., None]
    context = (
        context.transpose(0, 3, 1, 2, 4).reshape(models, length, query_width).astype(jnp.bfloat16)
    )
    attended = jnp.einsum(
        "mtc,mcd->mtd",
        lax.all_gather(context, "head", axis=2, tiled=True),
        out_weight,
        preferred_element_type=jnp.float32,
    )
    return attended.astype(jnp.bfloat16)


def solution(mesh):
    return jax.shard_map(
        local,
        mesh=mesh,
        in_specs=(
            P(None, "ctx", "head"),
            P(None, "ctx", "head"),
            P(None, "ctx", "head"),
            P("ctx"),
            P(None, None, "head"),
        ),
        out_specs=P(None, "ctx", "head"),
        check_vma=False,
    )
```

profile of v0, /device:TPU:1, one launch (start us, length us, event | category | flops | bytes accessed | tf_op | source)
XLA Modules:
  0.0 409.3 jit_solution(14812470316874369524)
XLA Ops:
  14.7 86.9 %all-gather.6.cloned.1.call-done = bf16[2,10240,256]{2,0,1:T(2,128)(2,1)} async-done(((bf16[2,160,256]{2,0,1:T(2,128)(2,1)}), bf16[2,10240,256]{2,0,1:T(2,128)(2,1)}) %all-gather.6.cloned.1.call-update) | async-done | bytes 10485776 | tf_op jit(solution)/shard_map/all_gather | solution.py:111
  101.6 88.6 %all-gather.4.cloned.1.call-done = bf16[2,10240,256]{2,0,1:T(2,128)(2,1)} async-done(((bf16[2,160,256]{2,0,1:T(2,128)(2,1)}), bf16[2,10240,256]{2,0,1:T(2,128)(2,1)}) %all-gather.4.cloned.1.call-update) | async-done | bytes 10485776 | tf_op jit(solution)/shard_map/all_gather | solution.py:110
  190.3 174.5 %while.21 = (s32[]{:T(128)}, f32[2,2,4,160]{3,2,1,0:T(4,128)S(1)}, f32[2,2,4,160]{3,2,1,0:T(4,128)S(1)}, f32[2,2,4,160,128]{4,3,2,1,0:T(8,128)}, s32[160]{0:T(25...) while((s32[]{:T(128)}, f32[2,2,4,160]{3,2,1,0:T(4,128)S(1)}, ...), condition=%wide.wide.region_3.4_spmd.clone, body=%wide.wide.region_0.3_spmd.clone.sunk | while | flops 858503360 | bytes 40967304 | solution.py:102
  190.5 2.2 constant_dynamic-slice_fusion.4
  196.2 2.0 fusion.51
  201.4 2.2 constant_dynamic-slice_fusion.4
  207.1 2.0 fusion.51
  212.3 2.2 constant_dynamic-slice_fusion.4
  218.0 2.0 fusion.51
  223.2 2.2 constant_dynamic-slice_fusion.4
  234.1 2.2 constant_dynamic-slice_fusion.4
  245.0 2.2 constant_dynamic-slice_fusion.4
  255.9 2.2 constant_dynamic-slice_fusion.4
  266.8 2.2 constant_dynamic-slice_fusion.4
  277.7 2.2 constant_dynamic-slice_fusion.4
  288.6 2.2 constant_dynamic-slice_fusion.4
  299.5 2.2 constant_dynamic-slice_fusion.4
  310.4 2.2 constant_dynamic-slice_fusion.4
  321.3 2.2 constant_dynamic-slice_fusion.4
  332.2 2.2 constant_dynamic-slice_fusion.4
  343.1 2.2 constant_dynamic-slice_fusion.4
  354.0 2.2 constant_dynamic-slice_fusion.4
  368.2 24.5 %all-gather.8.cloned.1.call-done = bf16[2,160,2048]{2,1,0:T(8,128)(2,1)} async-done(((bf16[2,160,1024]{2,1,0:T(8,128)(2,1)}), bf16[2,160,2048]{2,1,0:T(8,128)(2,1)}) %all-gather.8.cloned.1.call-update) | async-done | bytes 1310736 | tf_op jit(solution)/shard_map/all_gather | solution.py:122
  392.6 10.1 %convolution_convert_fusion = bf16[2,160,2048]{2,1,0:T(8,128)(2,1)} fusion(bf16[2,160,2048]{2,1,0:T(8,128)(2,1)} %all-gather.8.cloned.1.call-done, bf16[2,2048,2048]{2,1,0:T(8,128)(2,1)} %param.13), kind=kOutput, calls=%fused_computation.35 | convolution fusion | flops 2685009920 | bytes 19398656 | tf_op jit(solution)/shard_map/mtc,mcd->mtd/dot_general | solution.py:120
  (267 shorter events, 143.5 us)
Async XLA Ops:
  6.5 95.1 %all-gather.6.cloned.1.call-start = ((), (), s32[]{:S(2)}) async-start(), calls=%async_computation.1 | async-start | bytes 10649600 | tf_op jit(solution)/shard_map/all_gather | solution.py:111
  8.3 181.9 %all-gather.4.cloned.1.call-start = ((), (), s32[]{:S(2)}) async-start(), calls=%async_computation | async-start | bytes 10649600 | tf_op jit(solution)/shard_map/all_gather | solution.py:110
  11.4 381.2 %all-gather.8.cloned.1.call-start = ((), (), s32[]{:S(2)}) async-start(), calls=%async_computation.2 | async-start | bytes 1966080 | tf_op jit(solution)/shard_map/all_gather | solution.py:122
  11.5 178.7 %copy-start.3 = (s32[160]{0:T(256)S(1)}, s32[160]{0:T(256)}, u32[]{:S(2)}) copy-start(s32[160]{0:T(256)} %param.12) | copy-start | bytes 1924
  14.2 176.1 %copy-start = (bf16[2,160,1024]{2,1,0:T(8,128)(2,1)}, bf16[2,160,1024]{2,1,0:T(8,128)(2,1)S(1)}, u32[]{:S(2)}) copy-start(bf16[2,160,1024]{2,1,0:T(8,128)(2,1)S(1)} %copy.26) | copy-start | bytes 1966084
  194.5 3.7 copy-start.1
  200.1 1.1 copy-start.2
  205.4 3.7 copy-start.1
  211.0 1.1 copy-start.2
  216.4 3.7 copy-start.1
  227.3 3.7 copy-start.1
  238.2 3.7 copy-start.1
  249.1 3.7 copy-start.1
  260.0 3.7 copy-start.1
  265.5 1.1 copy-start.2
  270.9 3.7 copy-start.1
  281.8 3.7 copy-start.1
  292.7 3.7 copy-start.1
  303.6 3.7 copy-start.1
  314.5 3.7 copy-start.1
  325.4 3.7 copy-start.1
  336.3 3.7 copy-start.1
  347.2 3.7 copy-start.1
  358.1 3.7 copy-start.1
  (13 other events, 13.8 us)
Sparse Core Ops, SparseCore 0:
  10.6 91.0 all-gather.5
  104.8 85.3 all-gather.3
  368.3 24.3 all-gather.7
where the time goes:
time: 410 us; the launch traced here: 409 us
  waiting for transfers between devices  200 us (49%)
  local copies, waits for them, and re-layouts  89.5 us (22%)
  matrix products  65.6 us (16%)
  other arithmetic  39.4 us (10%)
  between operations  13.2 us (3%)
    all_gather x1, waiting for transfers between devices, local(): lax.all_gather(keys_rot, 'ctx', axis=1, tiled=True)  88.6 us
    all_gather x1, waiting for transfers between devices, local(): lax.all_gather(values, 'ctx', axis=1, tiled=True)  86.9 us
    dynamic_slice x32, local copies, waits for them, and re-layouts, one_span(): value_block = lax.dynamic_slice_in_dim(value_piece, offset, span, 1)  50.1 us
    reduce_sum x16, other arithmetic, attend_block(): running_sum = running_sum * rescale + jnp.sum(weights, axis=-1)  32.5 us
    dot_general x16, matrix products, attend_block(): jnp.einsum('mgrtk,mkgd->mgrtd', weights.astype(jnp.bfloat16), value_view,...  29 us
    dot_general x16, matrix products, attend_block(): jnp.einsum('mtgrd,mkgd->mgrtk', query_view, key_view, preferred_element_t...  26.5 us
    all_gather x1, waiting for transfers between devices, local(): lax.all_gather(context, 'head', axis=2, tiled=True)  24.5 us
    while x80, local copies, waits for them, and re-layouts  16.8 us
  transfers between devices with their start and end apart: 3, of which 3 were waited for; matrix products, arithmetic and copies ran while one was open for 1% of the time, Pallas kernels for 0%

commit v1 on v0

v1 whole, which is shorter than its diff:
```python
import functools

import jax
import jax.numpy as jnp
import numpy as np
from jax import lax
from jax.experimental import pallas as pl
from jax.experimental.pallas import tpu as pltpu
from jax.sharding import PartitionSpec as P

MESH = pl.DeviceIdType.MESH
HD = 128
NY, NZ = 4, 4
TOK = 160
STRIPES = 64
GROUP = 4
TILE = 16
BLOCKS = TOK // TILE
KEYS = TILE * STRIPES
ROWS = NY * GROUP * TILE
LOW = -1e30
LOG2E = 1.4426950408889634


def place():
    c = lax.axis_index("ctx")
    return c // 32, (c // 8) % NY, (c // 2) % NZ, c % 2, lax.axis_index("head")


def index(xh, y, z, core):
    return ((xh * NY + y) * NZ + z) * 2 + core


def enter(partners):
    barrier = pltpu.get_barrier_semaphore()
    for device in partners:
        pl.semaphore_signal(barrier, inc=1, device_id=device, device_id_type=MESH)
    return barrier


def rotated(x, cosine, sine):
    x = x.astype(jnp.float32)
    return (x * cosine + pltpu.roll(x, 64, 1) * sine).astype(jnp.bfloat16)


def gather_kernel(
    freq_ref, q_ref, k_ref, v_ref, doc_ref, kv, q_out, doc_out,
    stage, xstage, qstage, tables, send, recv, xrecv, qrecv, drecv, local,
):
    xh, y, z, core, head = place()
    me = index(xh, y, z, core)
    xpart = index(1 - xh, y, z, core)
    ypeer = [index(xh, (y + d) % NY, z, core) for d in range(NY)]
    zup, zdown = index(xh, y, (z + 1) % NZ, core), index(xh, y, (z + 3) % NZ, core)
    sibling = index(xh, y, z, 1 - core)
    partners = [xpart, ypeer[1], ypeer[2], ypeer[3], zup, zdown, sibling]
    barrier = enter([(p, head) for p in partners])

    positions = lax.broadcasted_iota(jnp.int32, (TOK, HD), 0) * STRIPES + me
    angles = positions.astype(jnp.float32) * freq_ref[...]
    first = lax.broadcasted_iota(jnp.int32, (TOK, HD), 1) < HD // 2
    sine = jnp.sin(angles)
    tables[0] = jnp.cos(angles)
    tables[1] = jnp.where(first, -sine, sine)

    for p in range(4):
        cols = pl.ds(p % 2 * HD, HD)
        stage[p, 0] = rotated(k_ref[p // 2, :, cols], tables[0], tables[1])
        stage[p, 1] = v_ref[p // 2, :, cols]
    pl.semaphore_wait(barrier, len(partners))

    started = []

    def push(src, dst, sem, device):
        copy = pltpu.make_async_remote_copy(
            src_ref=src, dst_ref=dst, send_sem=send.at[len(started)], recv_sem=sem,
            device_id=(device, head), device_id_type=MESH,
        )
        copy.start()
        started.append(copy)

    def arrived(dst, sem):
        pltpu.make_async_remote_copy(
            src_ref=dst, dst_ref=dst, send_sem=send.at[0], recv_sem=sem,
            device_id=(sibling, head), device_id_type=MESH,
        ).wait_recv()

    def slot(k, zz, cc):
        return index(xh if k < 4 else 1 - xh, (y + k) % NY, zz, cc)

    def forward(s, device):
        push(kv.at[s], kv.at[s], recv.at[s], device)

    def take(k, zz):
        s = slot(k, zz, core)
        arrived(kv.at[s], recv.at[s])
        return s

    own = stage.at[y]
    push(own, kv.at[me], recv.at[me], zup)
    push(own, kv.at[me], recv.at[me], zdown)
    push(own, kv.at[me], recv.at[me], xpart)
    for d in (2, 1, 3):
        push(stage.at[(y + d) % NY], kv.at[me], recv.at[me], ypeer[d])
    for d in (1, 2, 3):
        push(stage.at[(y + d) % NY], xstage.at[d - 1], xrecv.at[d - 1], xpart)
    push(own, kv.at[me], recv.at[me], sibling)
    own_copy = pltpu.make_async_copy(own, kv.at[me], local.at[0])
    own_copy.start()

    for p in range(4):
        for r in range(GROUP):
            cols = pl.ds((p % 2 * GROUP + r) * HD, HD)
            qstage[p, :, pl.ds(r * HD, HD)] = rotated(q_ref[p // 2, :, cols], tables[0], tables[1])
    q_copy = pltpu.make_async_copy(qstage.at[y], q_out.at[y], local.at[1])
    q_copy.start()
    doc_copy = pltpu.make_async_copy(doc_ref, doc_out.at[y], local.at[2])
    doc_copy.start()

    zn, zp, zo = (z + 1) % NZ, (z + 3) % NZ, (z + 2) % NZ
    for k in range(8):
        if k > 0:
            s = take(k, z)
            forward(s, zup)
            forward(s, zdown)
            forward(s, sibling)
        s = take(k, zp)
        if k % 2 == 0:
            forward(s, zup)
        forward(s, sibling)
        s = take(k, zn)
        if k % 2 == 1:
            forward(s, zdown)
        forward(s, sibling)
        if k > 0:
            forward(take(k - 1, zo), sibling)
        if k == 2:
            for d in (1, 2, 3):
                arrived(xstage.at[d - 1], xrecv.at[d - 1])
                push(xstage.at[d - 1], kv.at[xpart], recv.at[xpart], ypeer[d])
            for d in (2, 1, 3):
                push(qstage.at[(y + d) % NY], q_out.at[y], qrecv.at[y], ypeer[d])
                push(doc_ref, doc_out.at[y], drecv.at[y], ypeer[d])
    forward(take(7, zo), sibling)
    for k in range(8):
        for zz in (z, zp, zn, zo):
            s = slot(k, zz, 1 - core)
            arrived(kv.at[s], recv.at[s])
    for d in (1, 2, 3):
        p = (y + d) % NY
        arrived(q_out.at[p], qrecv.at[p])
        arrived(doc_out.at[p], drecv.at[p])
    own_copy.wait()
    q_copy.wait()
    doc_copy.wait()
    for copy in started:
        copy.wait_send()


def gather(freq, q, k, v, doc):
    vmem = pl.BlockSpec(memory_space=pltpu.VMEM)
    hbm = pl.BlockSpec(memory_space=pl.ANY)
    dma = pltpu.SemaphoreType.DMA
    return pl.pallas_call(
        gather_kernel,
        out_shape=(
            jax.ShapeDtypeStruct((STRIPES, 2, TOK, HD), jnp.bfloat16),
            jax.ShapeDtypeStruct((NY, TOK, GROUP * HD), jnp.bfloat16),
            jax.ShapeDtypeStruct((NY, TOK, HD), jnp.int32),
        ),
        in_specs=[vmem] * 5,
        out_specs=(hbm, hbm, hbm),
        scratch_shapes=[
            pltpu.VMEM((4, 2, TOK, HD), jnp.bfloat16),
            pltpu.VMEM((3, 2, TOK, HD), jnp.bfloat16),
            pltpu.VMEM((4, TOK, GROUP * HD), jnp.bfloat16),
            pltpu.VMEM((2, TOK, HD), jnp.float32),
            dma((96,)),
            dma((STRIPES,)),
            dma((3,)),
            dma((NY,)),
            dma((NY,)),
            dma((3,)),
        ],
        compiler_params=pltpu.CompilerParams(
            collective_id=0, has_side_effects=True, vmem_limit_bytes=32 * 2**20
        ),
    )(freq, q, k, v, doc)


def attend_kernel(kv_hbm, q_ref, doc_ref, out_ref, kbuf, vbuf, qbuf, top, total, acc, sem):
    xh, y, z, core, _ = place()
    copies = []
    for j in range(BLOCKS):
        rows = pl.ds(j * TILE, TILE)
        pair = (
            pltpu.make_async_copy(kv_hbm.at[:, 0, rows], kbuf.at[j], sem.at[0, j]),
            pltpu.make_async_copy(kv_hbm.at[:, 1, rows], vbuf.at[j], sem.at[1, j]),
        )
        for copy in pair:
            copy.start()
        copies.append(pair)

    lane = lax.broadcasted_iota(jnp.int32, (1, KEYS), 1)
    key_at = (lane % TILE) * STRIPES + lane // TILE
    scale = HD**-0.5 * LOG2E

    for i in range(BLOCKS):
        for copy in copies[i]:
            copy.wait()
        rows = pl.ds(i * TILE, TILE)
        docs = doc_ref[:, rows, :]
        low_doc = jnp.min(docs.astype(jnp.float32)).astype(jnp.int32)
        high_doc = jnp.max(docs.astype(jnp.float32)).astype(jnp.int32)
        for src in range(NY):
            for r in range(GROUP):
                at = (src * GROUP + r) * TILE
                qbuf[pl.ds(at, TILE), :] = q_ref[src, rows, pl.ds(r * HD, HD)]
        top[...] = jnp.full_like(top, LOW)
        total[...] = jnp.zeros_like(total)
        acc[...] = jnp.zeros_like(acc)

        def step(j, masked):
            keys = kbuf[j].reshape(KEYS, HD)
            values = vbuf[j].reshape(KEYS, HD)
            scores = lax.dot_general(
                qbuf[...], keys, (((1,), (1,)), ((), ())), preferred_element_type=jnp.float32
            ) * scale
            if masked:
                key_pos = key_at + j * (TILE * STRIPES)
                allowed = []
                for src in range(NY):
                    t = lax.broadcasted_iota(jnp.int32, (TILE, 1), 0) + i * TILE
                    q_pos = t * STRIPES + index(xh, src, z, core)
                    doc = docs[src][:, :1]
                    ok = (key_pos <= q_pos) & (key_pos >= doc)
                    allowed.extend([ok] * GROUP)
                parts = [
                    jnp.where(ok, scores[n * TILE : (n + 1) * TILE], LOW)
                    for n, ok in enumerate(allowed)
                ]
                scores = jnp.concatenate(parts, axis=0)
            before = top[:, :1]
            now = jnp.maximum(before, jnp.max(scores, axis=1, keepdims=True))
            weights = jnp.exp2(scores - now)
            shrink = jnp.exp2(before - now)
            top[...] = jnp.broadcast_to(now, top.shape)
            total[...] = total[...] * shrink + jnp.sum(weights, axis=1, keepdims=True)
            acc[...] = acc[...] * shrink + jnp.dot(
                weights.astype(jnp.bfloat16), values, preferred_element_type=jnp.float32
            )

        def one(j, _):
            needs = (j == i) | (j * KEYS < high_doc)

            @pl.when(needs)
            def _():
                step(j, True)

            @pl.when(jnp.logical_not(needs))
            def _():
                step(j, False)

            return 0

        lax.fori_loop(low_doc // KEYS, i + 1, one, 0)
        context = (acc[...] / total[...]).astype(jnp.bfloat16)
        for src in range(NY):
            for r in range(GROUP):
                at = (src * GROUP + r) * TILE
                out_ref[src, rows, pl.ds(r * HD, HD)] = context[at : at + TILE]


def attend(kv, q, doc):
    vmem = pl.BlockSpec(memory_space=pltpu.VMEM)
    return pl.pallas_call(
        attend_kernel,
        out_shape=jax.ShapeDtypeStruct((NY, TOK, GROUP * HD), jnp.bfloat16),
        in_specs=[pl.BlockSpec(memory_space=pl.ANY), vmem, vmem],
        out_specs=vmem,
        scratch_shapes=[
            pltpu.VMEM((BLOCKS, STRIPES, TILE, HD), jnp.bfloat16),
            pltpu.VMEM((BLOCKS, STRIPES, TILE, HD), jnp.bfloat16),
            pltpu.VMEM((ROWS, HD), jnp.bfloat16),
            pltpu.VMEM((ROWS, HD), jnp.float32),
            pltpu.VMEM((ROWS, HD), jnp.float32),
            pltpu.VMEM((ROWS, HD), jnp.float32),
            pltpu.SemaphoreType.DMA((2, BLOCKS)),
        ],
        compiler_params=pltpu.CompilerParams(vmem_limit_bytes=48 * 2**20),
    )(kv, q, doc)


def project_kernel(ctx, w, out_ref, cbuf, wbuf, acc, send, recv, wsem, local):
    xh, y, z, core, head = place()
    ypeer = [index(xh, (y + d) % NY, z, core) for d in range(NY)]
    others = [(ypeer[d], 1 - head) for d in range(NY)] + [(ypeer[d], head) for d in (1, 2, 3)]
    barrier = enter(others)
    order = [(head, (y + d) % NY) for d in range(NY)] + [(1 - head, (y + d) % NY) for d in range(NY)]
    fetches = []
    for n, (hh, p) in enumerate(order):
        rows = pl.ds(pl.multiple_of(hh * 1024 + p % 2 * 512, 512), 512)
        fetch = pltpu.make_async_copy(w.at[p // 2, rows], wbuf.at[n], wsem.at[n])
        fetches.append(fetch)
    mine = pltpu.make_async_copy(ctx.at[y], cbuf.at[head * 4 + y], local)
    mine.start()
    pl.semaphore_wait(barrier, len(others))
    started = []
    for hh, ds in ((1 - head, (2, 1, 3, 0)), (head, (2, 1, 3))):
        for d in ds:
            copy = pltpu.make_async_remote_copy(
                src_ref=ctx.at[(y + d) % NY],
                dst_ref=cbuf.at[head * 4 + y],
                send_sem=send.at[len(started)],
                recv_sem=recv.at[head * 4 + y],
                device_id=(ypeer[d], hh),
                device_id_type=MESH,
            )
            copy.start()
            started.append(copy)
    for fetch in fetches:
        fetch.start()
    acc[...] = jnp.zeros_like(acc)
    for n, (hh, p) in enumerate(order):
        at = hh * 4 + p
        fetches[n].wait()
        if n == 0:
            mine.wait()
        else:
            pltpu.make_async_remote_copy(
                src_ref=cbuf.at[at], dst_ref=cbuf.at[at], send_sem=send.at[0], recv_sem=recv.at[at],
                device_id=others[0], device_id_type=MESH,
            ).wait_recv()

        def tile(b, _):
            cols = pl.ds(pl.multiple_of(b * 512, 512), 512)
            acc[p // 2, :, cols] += jnp.dot(
                cbuf[at], wbuf[n, :, cols], preferred_element_type=jnp.float32
            )
            return 0

        lax.fori_loop(0, 4, tile, 0)
    out_ref[...] = acc[...].astype(jnp.bfloat16)
    for copy in started:
        copy.wait_send()


def project(ctx, w):
    hbm = pl.BlockSpec(memory_space=pl.ANY)
    dma = pltpu.SemaphoreType.DMA
    width = w.shape[2]
    return pl.pallas_call(
        project_kernel,
        out_shape=jax.ShapeDtypeStruct((2, TOK, width), jnp.bfloat16),
        in_specs=[hbm, hbm],
        out_specs=pl.BlockSpec(memory_space=pltpu.VMEM),
        scratch_shapes=[
            pltpu.VMEM((8, TOK, GROUP * HD), jnp.bfloat16),
            pltpu.VMEM((8, GROUP * HD, width), jnp.bfloat16),
            pltpu.VMEM((2, TOK, width), jnp.float32),
            dma((7,)),
            dma((8,)),
            dma((8,)),
            dma,
        ],
        compiler_params=pltpu.CompilerParams(
            collective_id=1, has_side_effects=True, vmem_limit_bytes=48 * 2**20
        ),
    )(ctx, w)


def local(queries, keys, values, doc_start, out_weight):
    freq = np.power(500000.0, -np.arange(HD // 2) * 2.0 / HD).astype(np.float32)
    freq = jnp.asarray(np.concatenate([freq, freq])[None, :])
    doc = jnp.broadcast_to(doc_start[:, None], (TOK, HD))
    kv, q, docs = gather(freq, queries, keys, values, doc)
    context = attend(kv, q, docs)
    return project(context, out_weight)


def solution(mesh):
    return jax.shard_map(
        local,
        mesh=mesh,
        in_specs=(
            P(None, "ctx", "head"),
            P(None, "ctx", "head"),
            P(None, "ctx", "head"),
            P("ctx"),
            P(None, None, "head"),
        ),
        out_specs=P(None, "ctx", "head"),
        check_vma=False,
    )
```

time: 410 us -> 107 us (0.26)
  waiting for transfers between devices: 200 us -> 0 us
  Pallas kernels: 0 us -> 99 us
  local copies, waits for them, and re-layouts: 89.5 us -> 7.67 us
  matrix products: 65.6 us -> 0 us
  other arithmetic: 39.4 us -> 0 us
  between operations: 13.2 us -> 0.05 us
    all_gather x3 -> x0, waiting for transfers between devices: 200 us -> none  [the longest x1 88.6 us: local(): lax.all_gather(keys_rot, 'ctx', axis=1, tiled=True)]
    pallas_call x0 -> x3, Pallas kernels: none -> 99 us  [the longest x1 48 us: gather(): pl.pallas_call(gather_kernel, out_shape=(jax.ShapeDtypeStruct((STRIPES, 2...]
    dot_general x33 -> x0, matrix products: 65.6 us -> none  [the longest x16 29 us: attend_block(): jnp.einsum('mgrtk,mkgd->mgrtd', weights.astype(jnp.bfloat16), value_view,...]
    dynamic_slice x48 -> x0, local copies, waits for them, and re-layouts: 65.1 us -> none  [the longest x32 50.1 us: one_span(): value_block = lax.dynamic_slice_in_dim(value_piece, offset, span, 1)]
    reduce_sum x16 -> x0, other arithmetic: 32.5 us -> none  [attend_block(): running_sum = running_sum * rescale + jnp.sum(weights, axis=-1)]
    while x80 -> x0, local copies, waits for them, and re-layouts: 16.8 us -> none
  transfers between devices with their start and end apart: 3 -> 0, of which waited for: 3 -> 0; matrix products, arithmetic and copies ran while one was open for 1% -> 0% of each run, Pallas kernels for 0% -> 0%
where the time goes in v1:
time: 107 us
  Pallas kernels  99 us (93%)
  local copies, waits for them, and re-layouts  7.67 us (7%)
    pallas_call x1, Pallas kernels, gather(): pl.pallas_call(gather_kernel, out_shape=(jax.ShapeDtypeStruct((STRIPES, 2...  48 us
    pallas_call x1, Pallas kernels, project(): pl.pallas_call(project_kernel, out_shape=jax.ShapeDtypeStruct((2, TOK, wi...  27.5 us
    pallas_call x1, Pallas kernels, attend(): pl.pallas_call(attend_kernel, out_shape=jax.ShapeDtypeStruct((NY, TOK, GR...  23.5 us
    unnamed x11, local copies, waits for them, and re-layouts  6.92 us

profile of v1, /device:TPU:1, one launch (start us, length us, event | category | flops | bytes accessed | tf_op | source)
XLA Modules:
  0.0 106.7 jit_solution(18065183923090573419)
XLA Ops:
  0.0 0.8 broadcast_in_dim.2.doc_ref
  0.8 0.0 copy-start.1
  0.8 1.1 %copy-done.1 = bf16[2,160,1024]{2,1,0:T(8,128)(2,1)S(1)} copy-done((bf16[2,160,1024]{2,1,0:T(8,128)(2,1)S(1)}, bf16[2,160,1024]{2,1,0:T(8,128)(2,1)}, u32[]{:S(2)}) %copy-start.1) | copy-done | bytes 655384
  1.9 0.0 copy-start.2
  1.9 0.9 copy-done.2
  2.8 0.0 copy-start.3
  2.8 0.9 copy-done.3
  3.7 0.0 copy-start.4
  3.7 0.7 copy-done.4
  4.3 48.0 %shard_map.64 = (bf16[64,2,160,128]{3,2,1,0:T(8,128)(2,1)S(1)}, bf16[4,160,512]{2,1,0:T(8,128)(2,1)S(1)}, s32[4,160,128]{2,1,0:T(8,128)S(1)}) custom-call(f32[1,128]{1,0:T(1,128)S(1)} %copy-done.4, bf16[2,160,1024]{2,1,0:T(8,128)(2,1)S(1)} %copy-done.1, bf16[2,160,256]{2,1,0:T(8,128)(2,1)S(1)} %copy-done.2, bf16[2,160,256]{2,1,0:T(8,128)(2,1)S(1)} %copy-done.3, ...), custom_call_target="tpu_custom_call" | custom-call | tf_op jit(solution)/shard_map/pallas_call | solution.py:164
  52.4 0.0 copy-start
  52.4 2.3 %copy-done = bf16[64,2,160,128]{3,2,1,0:T(8,128)(2,1)} copy-done((bf16[64,2,160,128]{3,2,1,0:T(8,128)(2,1)}, bf16[64,2,160,128]{3,2,1,0:T(8,128)(2,1)S(1)}, u32[]{:S(2)}) %copy-start) | copy-done | bytes 5242904
  54.7 23.5 %shard_map.65.ctx = bf16[4,160,512]{2,1,0:T(8,128)(2,1)S(1)} custom-call(bf16[64,2,160,128]{3,2,1,0:T(8,128)(2,1)} %copy-done, bf16[4,160,512]{2,1,0:T(8,128)(2,1)S(1)} %get-tuple-element.9.q_ref, s32[4,160,128]{2,1,0:T(8,128)S(1)} %get-tuple-element.10.doc_ref), custom_call_target="tpu_custom_call" | custom-call | tf_op jit(solution)/shard_map/pallas_call | solution.py:276
  78.2 27.5 %shard_map.66 = bf16[2,160,2048]{2,1,0:T(8,128)(2,1)S(1)} custom-call(bf16[4,160,512]{2,1,0:T(8,128)(2,1)S(1)} %shard_map.65.ctx, bf16[2,2048,2048]{2,1,0:T(8,128)(2,1)} %w.1), custom_call_target="tpu_custom_call" | custom-call | tf_op jit(solution)/shard_map/pallas_call | solution.py:352
  105.7 1.1 copy.8
Async XLA Ops:
  0.8 1.1 %copy-start.1 = (bf16[2,160,1024]{2,1,0:T(8,128)(2,1)S(1)}, bf16[2,160,1024]{2,1,0:T(8,128)(2,1)}, u32[]{:S(2)}) copy-start(bf16[2,160,1024]{2,1,0:T(8,128)(2,1)} %q_ref.1) | copy-start | bytes 1966084
  1.9 0.9 copy-start.2
  2.8 0.9 copy-start.3
  3.7 0.7 copy-start.4
  52.4 2.3 %copy-start = (bf16[64,2,160,128]{3,2,1,0:T(8,128)(2,1)}, bf16[64,2,160,128]{3,2,1,0:T(8,128)(2,1)S(1)}, u32[]{:S(2)}) copy-start(bf16[64,2,160,128]{3,2,1,0:T(8,128)(2,1)S(1)} %get-tuple-element.8.kv_hbm) | copy-start | bytes 15728644

commit v2 on v0

v2 whole, which is shorter than its diff:
```python
import functools

import jax
import jax.numpy as jnp
import numpy as np
from jax import lax
from jax.experimental import pallas as pl
from jax.experimental.pallas import tpu as pltpu
from jax.sharding import PartitionSpec as P

MESH = pl.DeviceIdType.MESH
HD = 128
NY, NZ = 4, 4
TOK = 160
STRIPES = 64
GROUP = 4
WIDE = GROUP * HD
TILE = 16
BLOCKS = TOK // TILE
KEYS = TILE * STRIPES
ROWS = NY * GROUP * TILE
CHUNKS = 5
CT = TOK // CHUNKS
UNIT = 256
UNITS = KEYS // UNIT
LEAD = 3
LAST = 8320
LOW = -1e30
BIG = 2.0**40
SCALE = HD**-0.5 * 1.4426950408889634
SUMS = 16


def index(xh, y, z, core):
    return ((xh * NY + y) * NZ + z) * 2 + core


def rotated(x, cosine, sine):
    x = x.astype(jnp.float32)
    return (x * cosine + pltpu.roll(x, 64, 1) * sine).astype(jnp.bfloat16)


def first_key_block(i):
    return i // (LAST // KEYS + 1) * (LAST // KEYS)


def kernel(
    freq_ref, doc_ref, q_ref, k_ref, v_ref, w_ref, out_ref,
    kv, stage, qst, qall, docs, tables, dcol, kaug, causal, qbuf, vt,
    scores, tops, acc, ctx, cbuf, wbuf,
    ysend, yrecv, qsend, qrecv, dsend, drecv, zsend, zrecv, osend, orecv,
    bsend, brecv, csend, crecv, wsem,
):
    c_at = lax.axis_index("ctx")
    head = lax.axis_index("head")
    xh, y, z, core = c_at // 32, (c_at // 8) % NY, (c_at // 2) % NZ, c_at % 2
    xp = 1 - xh
    zup, zdown = (z + 1) % NZ, (z + 3) % NZ
    zfar = (z + 2) % NZ
    ys = [(y + d) % NY for d in range(NY)]
    peers = [(index(xh, ys[d], z, core), head) for d in range(NY)]
    across = [(index(xp, ys[d], z, core), head) for d in range(NY)]
    mirror = [(index(xh, ys[d], z, core), 1 - head) for d in range(NY)]
    above = (index(xh, y, zup, core), head)
    below = (index(xh, y, zdown, core), head)
    sibling = (index(xh, y, z, 1 - core), head)
    partners = peers[1:] + across + mirror + [above, below, sibling]

    def remote(src, dst, send, recv, device):
        return pltpu.make_async_remote_copy(
            src_ref=src, dst_ref=dst, send_sem=send, recv_sem=recv,
            device_id=device, device_id_type=MESH,
        )

    def arrived(ref, sem):
        remote(ref, ref, wsem.at[0], sem, sibling).wait_recv()

    def group(c, zz, cc, low=0, size=8):
        return kv.at[c, pl.ds((cc * NZ + zz) * 8 + low, size)]

    slot = (core * NZ + z) * 8 + xh * NY + y

    def chunk(c):
        return pl.ds(pl.multiple_of(c * CT, CT), CT)

    def key_copies(c):
        made = []
        for n, (d, device) in enumerate(
            [(0, across[0])] + [(d, t[d]) for d in (2, 1, 3) for t in (peers, across)]
        ):
            made.append(
                remote(stage.at[c, ys[d]], kv.at[c, slot], ysend.at[c, n], yrecv.at[c], device)
            )
        return made

    def query_copies(c):
        return [
            remote(
                qst.at[ys[d], chunk(c)], qall.at[y, chunk(c)], qsend.at[c, d - 1], qrecv.at[c],
                peers[d],
            )
            for d in (2, 1, 3)
        ]

    def doc_copies():
        return [
            remote(doc_ref, docs.at[y], dsend.at[d - 1], drecv.at[0], peers[d]) for d in (1, 2, 3)
        ]

    def near_copies(c):
        own = group(c, z, core)
        return [
            remote(own, own, zsend.at[c, 0], zrecv.at[c, 0], above),
            remote(own, own, zsend.at[c, 1], zrecv.at[c, 1], below),
        ]

    def far_copies(c):
        up, down = group(c, zdown, core, 0, 4), group(c, zup, core, 4, 4)
        return [
            remote(up, up, osend.at[c, 0], orecv.at[c, 0], above),
            remote(down, down, osend.at[c, 1], orecv.at[c, 1], below),
        ]

    def sibling_copies(c, low=0, high=4):
        made = []
        for n, zz in list(enumerate((z, zdown, zup, zfar)))[low:high]:
            ref = group(c, zz, core)
            made.append(remote(ref, ref, bsend.at[c, n], brecv.at[c, n], sibling))
        return made

    def context_copies(c):
        made = []
        for n, (d, device) in enumerate(
            [(d, mirror[d]) for d in (2, 1, 3, 0)] + [(d, peers[d]) for d in (2, 1, 3)]
        ):
            made.append(
                remote(
                    ctx.at[ys[d], chunk(c)], cbuf.at[head * 4 + y, chunk(c)],
                    csend.at[c, n], crecv.at[head * 4 + y], device,
                )
            )
        return made

    def start(copies):
        for copy in copies:
            copy.start()

    barrier = pltpu.get_barrier_semaphore()
    for device in partners:
        pl.semaphore_signal(barrier, inc=1, device_id=device, device_id_type=MESH)

    positions = lax.broadcasted_iota(jnp.int32, (TOK, HD), 0) * STRIPES + c_at
    angles = positions.astype(jnp.float32) * freq_ref[...]
    lane = lax.broadcasted_iota(jnp.int32, (TOK, HD), 1)
    sine = jnp.sin(angles)
    tables[0] = jnp.cos(angles)
    tables[1] = jnp.where(lane < HD // 2, -sine, sine)
    for p in range(4):
        cols = pl.ds(p % 2 * HD, HD)
        turned = rotated(k_ref[p // 2, :, cols], tables[0], tables[1])
        held = v_ref[p // 2, :, cols]
        for c in range(CHUNKS):
            stage[c, p, 0] = turned[c * CT : (c + 1) * CT]
            stage[c, p, 1] = held[c * CT : (c + 1) * CT]
    pl.semaphore_wait(barrier, len(partners))

    def send_keys(c):
        start(key_copies(c))
        pltpu.make_async_copy(stage.at[c, y], kv.at[c, slot], yrecv.at[c]).start()

    def send_queries(c):
        start(query_copies(c))
        pltpu.make_async_copy(qst.at[y, chunk(c)], qall.at[y, chunk(c)], qrecv.at[c]).start()

    send_keys(0)
    start(doc_copies())
    pltpu.make_async_copy(doc_ref, docs.at[y], drecv.at[0]).start()
    send_keys(1)
    for p in range(4):
        for r in range(GROUP):
            cols = pl.ds((p % 2 * GROUP + r) * HD, HD)
            qst[p, :, pl.ds(r * HD, HD)] = rotated(q_ref[p // 2, :, cols], tables[0], tables[1])
    send_queries(0)
    for c in range(2, CHUNKS):
        send_keys(c)
        send_queries(c - 1)
    send_queries(CHUNKS - 1)
    weights_in = [
        pltpu.make_async_copy(w_ref.at[m], wbuf.at[m], wsem.at[1 + m]) for m in range(2)
    ]
    start(weights_in)

    def near(c):
        arrived(group(c, z, core), yrecv.at[c])
        start(near_copies(c))
        start(sibling_copies(c, 0, 1))

    def far(c):
        arrived(group(c, zdown, core), zrecv.at[c, 0])
        arrived(group(c, zup, core), zrecv.at[c, 1])
        start(far_copies(c))
        start(sibling_copies(c, 1, 3))

    def whole(c):
        arrived(group(c, zfar, core, 0, 4), orecv.at[c, 0])
        arrived(group(c, zfar, core, 4, 4), orecv.at[c, 1])
        start(sibling_copies(c, 3, 4))

    def other(c):
        for n, zz in enumerate((z, zdown, zup, zfar)):
            arrived(group(c, zz, 1 - core), brecv.at[c, n])

    near(0)

    row = lax.broadcasted_iota(jnp.int32, (KEYS, HD), 0)
    col = lax.broadcasted_iota(jnp.int32, (KEYS, HD), 1)
    s = row // TILE
    key_at = (row % TILE) * STRIPES + (s % 8 * NZ + s // 8 % NZ) * 2 + s // 32
    kind = col - 64
    query_at = (kind % TILE) * STRIPES + index(xh, kind // TILE, z, core)
    causal[0] = jnp.zeros((KEYS, HD), jnp.bfloat16)
    causal[1] = jnp.where((kind >= 0) & (key_at > query_at), 1.0, 0.0).astype(jnp.bfloat16)
    vt[:, HD:, :] = jnp.ones((BLOCKS, SUMS, KEYS), jnp.bfloat16)
    qbuf[BLOCKS] = jnp.zeros((ROWS, 2 * HD), jnp.bfloat16)

    near(1)

    arrived(docs, drecv.at[0])
    seen = docs[...].astype(jnp.float32)

    def highest(values):
        return jnp.max(jnp.max(values, axis=(0, 1)).reshape(1, -1), axis=1, keepdims=True)

    cut_a = highest(seen)
    cut_b = highest(jnp.where(seen < cut_a, seen, -1.0))
    cut_c = highest(jnp.where(seen < cut_b, seen, -1.0))
    one_lane = lax.broadcasted_iota(jnp.int32, (1, HD), 1)
    cuts = jnp.where(
        one_lane == 0, cut_a, jnp.where(one_lane == 1, cut_b, jnp.where(one_lane == 2, cut_c, -5.0))
    )
    for src in range(NY):
        line = seen[src]
        dcol[src, :HD] = jnp.broadcast_to(line[:1, :HD], (HD, HD)).T
        dcol[src, HD:] = jnp.broadcast_to(line[:1, HD:], (HD, HD)).T[: TOK - HD]
    key_pos = key_at.astype(jnp.float32)

    def key_mask(j, _):
        base = (j * KEYS).astype(jnp.float32)
        kaug[j] = jnp.where(key_pos + base < cuts, 1.0, 0.0).astype(jnp.bfloat16)
        return 0

    lax.fori_loop(0, BLOCKS, key_mask, 0)

    def tile(i):
        return pl.ds(pl.multiple_of(i * TILE, TILE), TILE)

    small_lane = lax.broadcasted_iota(jnp.int32, (TILE, HD), 1)
    small_row = lax.broadcasted_iota(jnp.int32, (TILE, HD), 0)

    def take_queries(c):
        arrived(qall.at[:, chunk(c)], qrecv.at[c])

        def one(n, _):
            i = c * 2 + n
            for src in range(NY):
                hit = (dcol[src, tile(i), :] == cuts) | (small_lane == 64 + src * TILE + small_row)
                mask = jnp.where(hit, -BIG, 0.0).astype(jnp.bfloat16)
                for r in range(GROUP):
                    at = pl.ds((src * GROUP + r) * TILE, TILE)
                    qbuf[i, at, :HD] = qall[src, tile(i), pl.ds(r * HD, HD)]
                    qbuf[i, at, HD:] = mask
            return 0

        lax.fori_loop(0, 2, one, 0)

    far(0)
    take_queries(0)
    whole(0)
    near(2)
    other(0)

    def score(i, j, h, first):
        slots = pl.ds(h * UNIT // TILE, UNIT // TILE)
        at = pl.ds(h * UNIT, UNIT)
        rows = pl.ds(pl.multiple_of(j % 2 * TILE, TILE), TILE)
        keys = kv[j // 2, slots, 0, rows, :].reshape(UNIT, HD)
        mask = kaug[j, at, :] + causal[(j + 1) // (i + 1), at, :]
        found = lax.dot_general(
            jnp.concatenate([keys, mask], axis=1), qbuf[i], (((1,), (1,)), ((), ())),
            preferred_element_type=jnp.float32,
        )
        scores[h] = found
        before = jnp.full((1, ROWS), LOW, jnp.float32) if first else tops[(h - 1) % UNITS, :1, :]
        now = jnp.maximum(before, jnp.max(found, axis=0, keepdims=True))
        tops[h, :1, :] = now
        tops[h, 1:2, :] = jnp.exp2((before - now) * SCALE)

    def absorb(j, h):
        top = tops[h, :1, :] * SCALE
        weights = jnp.exp2(scores[h] * SCALE - top).astype(jnp.bfloat16)
        acc[...] = acc[...] * tops[h, 1:2, :] + jnp.dot(
            vt[j, :, pl.ds(h * UNIT, UNIT)], weights, preferred_element_type=jnp.float32
        )

    acc[...] = jnp.zeros_like(acc)
    for h in range(LEAD):
        score(0, 0, h, h == 0)

    def block(i):
        def steps(j, next_i, next_j, last):
            for h in range(UNITS):
                if h + LEAD < UNITS:
                    score(i, j, h + LEAD, False)
                else:
                    score(next_i, next_j, h + LEAD - UNITS, last and h + LEAD == UNITS)
                absorb(j, h)

        def one(j, _):
            steps(j, i, j + 1, False)
            return 0

        lax.fori_loop(first_key_block(i), i, one, 0)
        steps(i, i + 1, first_key_block(i + 1) % BLOCKS, True)
        done = (acc[:HD, :] / acc[HD : HD + 1, :]).T.astype(jnp.bfloat16)
        acc[...] = jnp.zeros_like(acc)
        for src in range(NY):
            for r in range(GROUP):
                at = (src * GROUP + r) * TILE
                ctx[src, tile(i), pl.ds(r * HD, HD)] = done[at : at + TILE]

    def body(c, _):
        @pl.when(c < CHUNKS - 1)
        def _():
            take_queries(c + 1)

        def turn(n, _):
            j = c * 2 + n
            rows = pl.ds(pl.multiple_of(n * TILE, TILE), TILE)
            vt[j, :HD, :] = kv[c, :, 1, rows, :].reshape(KEYS, HD).T
            return 0

        lax.fori_loop(0, 2, turn, 0)
        block(c * 2)

        @pl.when(c < CHUNKS - 1)
        def _():
            far(c + 1)

        @pl.when(c < CHUNKS - 3)
        def _():
            near(c + 3)

        block(c * 2 + 1)
        start(context_copies(c))
        pltpu.make_async_copy(
            ctx.at[y, chunk(c)], cbuf.at[head * 4 + y, chunk(c)], crecv.at[head * 4 + y]
        ).start()

        @pl.when(c < CHUNKS - 1)
        def _():
            whole(c + 1)
            other(c + 1)

        return 0

    lax.fori_loop(0, CHUNKS, body, 0)

    for n in range(8):
        arrived(cbuf.at[n], crecv.at[n])
    for copy in weights_in:
        copy.wait()

    def project(n, _):
        m = n // 4
        cols = pl.ds(pl.multiple_of(n % 4 * 512, 512), 512)
        rows = jnp.concatenate([cbuf[hh * 4 + m * 2 + g] for hh in range(2) for g in range(2)], axis=1)
        out_ref[m, :, cols] = jnp.dot(
            rows, wbuf[m, :, cols], preferred_element_type=jnp.float32
        ).astype(jnp.bfloat16)
        return 0

    lax.fori_loop(0, 8, project, 0)

    for copy in doc_copies():
        copy.wait_send()

    def drain(c, _):
        for copy in (
            key_copies(c) + query_copies(c) + near_copies(c) + far_copies(c)
            + sibling_copies(c) + context_copies(c)
        ):
            copy.wait_send()
        return 0

    lax.fori_loop(0, CHUNKS, drain, 0)


def local(queries, keys, values, doc_start, out_weight):
    freq = np.power(500000.0, -np.arange(HD // 2) * 2.0 / HD).astype(np.float32)
    freq = jnp.asarray(np.concatenate([freq, freq])[None, :])
    doc = jnp.broadcast_to(jnp.pad(doc_start, (0, 256 - TOK))[None, :], (8, 256))
    width = out_weight.shape[2]
    vmem = pl.BlockSpec(memory_space=pltpu.VMEM)
    hbm = pl.BlockSpec(memory_space=pl.ANY)
    dma = pltpu.SemaphoreType.DMA
    b16, f32 = jnp.bfloat16, jnp.float32
    return pl.pallas_call(
        kernel,
        out_shape=jax.ShapeDtypeStruct((2, TOK, width), b16),
        in_specs=[vmem] * 5 + [hbm],
        out_specs=vmem,
        scratch_shapes=[
            pltpu.VMEM((CHUNKS, STRIPES, 2, CT, HD), b16),
            pltpu.VMEM((CHUNKS, 4, 2, CT, HD), b16),
            pltpu.VMEM((4, TOK, WIDE), b16),
            pltpu.VMEM((4, TOK, WIDE), b16),
            pltpu.VMEM((4, 8, 256), jnp.int32),
            pltpu.VMEM((2, TOK, HD), f32),
            pltpu.VMEM((4, TOK, HD), f32),
            pltpu.VMEM((BLOCKS, KEYS, HD), b16),
            pltpu.VMEM((2, KEYS, HD), b16),
            pltpu.VMEM((BLOCKS + 1, ROWS, 2 * HD), b16),
            pltpu.VMEM((BLOCKS, HD + SUMS, KEYS), b16),
            pltpu.VMEM((UNITS, UNIT, ROWS), f32),
            pltpu.VMEM((UNITS, 8, ROWS), f32),
            pltpu.VMEM((HD + SUMS, ROWS), f32),
            pltpu.VMEM((4, TOK, WIDE), b16),
            pltpu.VMEM((8, TOK, WIDE), b16),
            pltpu.VMEM((2, 2048, width), b16),
            dma((CHUNKS, 7)),
            dma((CHUNKS,)),
            dma((CHUNKS, 3)),
            dma((CHUNKS,)),
            dma((3,)),
            dma((1,)),
            dma((CHUNKS, 2)),
            dma((CHUNKS, 2)),
            dma((CHUNKS, 2)),
            dma((CHUNKS, 2)),
            dma((CHUNKS, 4)),
            dma((CHUNKS, 4)),
            dma((CHUNKS, 7)),
            dma((8,)),
            dma((3,)),
        ],
        compiler_params=pltpu.CompilerParams(
            collective_id=0, has_side_effects=True, vmem_limit_bytes=56 * 2**20
        ),
    )(freq, doc, queries, keys, values, out_weight)


def solution(mesh):
    return jax.shard_map(
        local,
        mesh=mesh,
        in_specs=(
            P(None, "ctx", "head"),
            P(None, "ctx", "head"),
            P(None, "ctx", "head"),
            P("ctx"),
            P(None, None, "head"),
        ),
        out_specs=P(None, "ctx", "head"),
        check_vma=False,
    )
```

time: 410 us -> 79.8 us (0.19)
  waiting for transfers between devices: 200 us -> 0 us
  local copies, waits for them, and re-layouts: 89.5 us -> 3.8 us
  Pallas kernels: 0 us -> 75.8 us
  matrix products: 65.6 us -> 0 us
  other arithmetic: 39.4 us -> 0 us
  between operations: 13.2 us -> 0.01 us
    all_gather x3 -> x0, waiting for transfers between devices: 200 us -> none  [the longest x1 88.6 us: local(): lax.all_gather(keys_rot, 'ctx', axis=1, tiled=True)]
    pallas_call x0 -> x1, Pallas kernels: none -> 75.8 us  [local(): pl.pallas_call(kernel, out_shape=jax.ShapeDtypeStruct((2, TOK, width), b1...]
    dot_general x33 -> x0, matrix products: 65.6 us -> none  [the longest x16 29 us: attend_block(): jnp.einsum('mgrtk,mkgd->mgrtd', weights.astype(jnp.bfloat16), value_view,...]
    dynamic_slice x48 -> x0, local copies, waits for them, and re-layouts: 65.1 us -> none  [the longest x32 50.1 us: one_span(): value_block = lax.dynamic_slice_in_dim(value_piece, offset, span, 1)]
    reduce_sum x16 -> x0, other arithmetic: 32.5 us -> none  [attend_block(): running_sum = running_sum * rescale + jnp.sum(weights, axis=-1)]
    while x80 -> x0, local copies, waits for them, and re-layouts: 16.8 us -> none
  transfers between devices with their start and end apart: 3 -> 0, of which waited for: 3 -> 0; matrix products, arithmetic and copies ran while one was open for 1% -> 0% of each run, Pallas kernels for 0% -> 0%
where the time goes in v2:
time: 79.8 us; the launch traced here: 79.6 us
  Pallas kernels  75.8 us (95%)
  local copies, waits for them, and re-layouts  3.8 us (5%)
    pallas_call x1, Pallas kernels, local(): pl.pallas_call(kernel, out_shape=jax.ShapeDtypeStruct((2, TOK, width), b1...  75.8 us
    unnamed x1, local copies, waits for them, and re-layouts  2.52 us

profile of v2, /device:TPU:1, one launch (start us, length us, event | category | flops | bytes accessed | tf_op | source)
XLA Modules:
  0.0 79.6 jit_solution(14436838381975940516)
XLA Ops:
  0.0 0.7 pad.4
  0.7 0.6 broadcast_in_dim.2.doc_ref
  1.3 75.8 %shard_map.64 = bf16[2,160,2048]{2,1,0:T(8,128)(2,1)} custom-call(f32[1,128]{1,0:T(1,128)} %constant.4.clone.freq_ref, s32[8,256]{1,0:T(8,128)} %broadcast_in_dim.2.doc_ref, bf16[2,160,1024]{2,1,0:T(8,128)(2,1)} %q_ref.1, bf16[2,160,256]{2,1,0:T(8,128)(2,1)} %k_ref.1, bf16[2,160,256]{2,1,0:T(8,128)(2,1)} %v_ref.1, bf16[2,2048,2048]{2,1,0:T(8,128)(2,1)} %w_ref.1), custom_call_target="tpu_custom_call" | custom-call | tf_op jit(solution)/shard_map/pallas_call | solution.py:407
  77.1 2.5 %copy.8 = bf16[2,160,2048]{2,1,0:T(8,128)(2,1)} copy(bf16[2,160,2048]{2,1,0:T(8,128)(2,1)} %shard_map.64) | data formatting | bytes 2621440

commit v3 on v2

v3 whole, which is shorter than its diff:
```python
import functools

import jax
import jax.numpy as jnp
import numpy as np
from jax import lax
from jax.experimental import pallas as pl
from jax.experimental.pallas import tpu as pltpu
from jax.sharding import PartitionSpec as P

MESH = pl.DeviceIdType.MESH
HD = 128
NY, NZ = 4, 4
TOK = 160
STRIPES = 64
GROUP = 4
WIDE = GROUP * HD
TILE = 16
BLOCKS = TOK // TILE
KEYS = TILE * STRIPES
ROWS = NY * GROUP * TILE
CHUNKS = 5
CT = TOK // CHUNKS
HALF = KEYS // 2
BUFFERS = 5
EARLY = 8 * TILE
LOW = -1e30
BIG = 2.0**40
SCALE = HD**-0.5 * 1.4426950408889634
SUMS = 16


def index(xh, y, z, core):
    return ((xh * NY + y) * NZ + z) * 2 + core


def rotated(x, cosine, sine):
    x = x.astype(jnp.float32)
    return (x * cosine + pltpu.roll(x, 64, 1) * sine).astype(jnp.bfloat16)


def kernel(
    freq_hbm, doc_hbm, q_hbm, k_hbm, v_hbm, w_ref, out_ref,
    freq_ref, doc_ref, q_ref, k_ref, v_ref, own_doc, kv, stage, qst, qall, docs, tables, dcol, kaug, causal, qbuf, vt,
    scores, tops, highs, acc, ctx, cbuf, wbuf,
    ysend, yrecv, qsend, qrecv, dsend, drecv, zsend, zrecv, osend, orecv,
    bsend, brecv, csend, crecv, wsem, isem,
):
    c_at = lax.axis_index("ctx")
    head = lax.axis_index("head")
    xh, y, z, core = c_at // 32, (c_at // 8) % NY, (c_at // 2) % NZ, c_at % 2
    xp = 1 - xh
    zup, zdown = (z + 1) % NZ, (z + 3) % NZ
    ys = [(y + d) % NY for d in range(NY)]
    peers = [(index(xh, ys[d], z, core), head) for d in range(NY)]
    across = [(index(xp, ys[d], z, core), head) for d in range(NY)]
    mirror = [(index(xh, ys[d], z, core), 1 - head) for d in range(NY)]
    above = (index(xh, y, zup, core), head)
    below = (index(xh, y, zdown, core), head)
    sibling = (index(xh, y, z, 1 - core), head)
    partners = peers[1:] + across + mirror + [above, below, sibling]

    def remote(src, dst, send, recv, device):
        return pltpu.make_async_remote_copy(
            src_ref=src, dst_ref=dst, send_sem=send, recv_sem=recv,
            device_id=device, device_id_type=MESH,
        )

    def arrived(ref, sem):
        remote(ref, ref, wsem.at[0], sem, sibling).wait_recv()

    def group(c, r, cc, low=0, size=8):
        return kv.at[c, pl.ds(r * 16 + cc * 8 + low, size)]

    slot = xh * NY + y

    def tile(i):
        return pl.ds(pl.multiple_of(i * TILE, TILE), TILE)

    def chunk(c):
        return pl.ds(pl.multiple_of(c * CT, CT), CT)

    def key_copies(c):
        made = []
        for n, (d, device) in enumerate(
            [(0, across[0])] + [(d, t[d]) for d in (2, 1, 3) for t in (peers, across)]
        ):
            made.append(
                remote(stage.at[c, ys[d]], kv.at[c, slot], ysend.at[c, n], yrecv.at[c], device)
            )
        return made

    def query_copies(c):
        return [
            remote(
                qst.at[ys[d], chunk(c)], qall.at[y, chunk(c)], qsend.at[c, d - 1], qrecv.at[c],
                peers[d],
            )
            for d in (2, 1, 3)
        ]

    def doc_copies():
        return [
            remote(own_doc, docs.at[y], dsend.at[d - 1], drecv.at[0], peers[d]) for d in (1, 2, 3)
        ]

    def near_copies(c):
        own = group(c, 0, 0)
        return [
            remote(own, group(c, 1, 0), zsend.at[c, 0], zrecv.at[c, 0], above),
            remote(own, group(c, 2, 0), zsend.at[c, 1], zrecv.at[c, 1], below),
        ]

    def far_copy(c, n):
        src, dst = group(c, 1 + n, 0, 4 * n, 4), group(c, 3, 0, 4 * n, 4)
        return remote(src, dst, osend.at[c, n], orecv.at[c, n], (above, below)[n])

    def sibling_copy(c, r):
        return remote(group(c, r, 0), group(c, r, 1), bsend.at[c, r], brecv.at[c, r], sibling)

    def context_copies(i):
        made = []
        part = i // 8
        for n, (d, device) in enumerate(
            [(d, mirror[d]) for d in (2, 1, 3, 0)] + [(d, peers[d]) for d in (2, 1, 3)]
        ):
            made.append(
                remote(
                    ctx.at[ys[d], tile(i)], cbuf.at[head * 4 + y, tile(i)],
                    csend.at[i, n], crecv.at[head * 4 + y, part], device,
                )
            )
        return made

    def send_context(i):
        start(context_copies(i))
        pltpu.make_async_copy(
            ctx.at[y, tile(i)], cbuf.at[head * 4 + y, tile(i)], crecv.at[head * 4 + y, i // 8]
        ).start()

    def start(copies):
        for copy in copies:
            copy.start()

    inputs = [
        pltpu.make_async_copy(src, dst, isem.at[n])
        for n, (src, dst) in enumerate(
            (
                (freq_hbm, freq_ref), (doc_hbm, doc_ref), (k_hbm, k_ref), (v_hbm, v_ref),
                (q_hbm, q_ref),
            )
        )
    ]
    start(inputs)
    barrier = pltpu.get_barrier_semaphore()
    for device in partners:
        pl.semaphore_signal(barrier, inc=1, device_id=device, device_id_type=MESH)

    positions = lax.broadcasted_iota(jnp.int32, (TOK, HD), 0) * STRIPES + c_at
    inputs[0].wait()
    angles = positions.astype(jnp.float32) * freq_ref[...]
    lane = lax.broadcasted_iota(jnp.int32, (TOK, HD), 1)
    sine = jnp.sin(angles)
    tables[0] = jnp.cos(angles)
    tables[1] = jnp.where(lane < HD // 2, -sine, sine)
    inputs[1].wait()
    own_doc[:, HD:] = jnp.zeros((8, HD), jnp.int32)
    own_doc[:1, :TOK] = doc_ref[...].reshape(1, TOK)
    inputs[2].wait()
    inputs[3].wait()
    for p in range(4):
        cols = pl.ds(p % 2 * HD, HD)
        turned = rotated(k_ref[p // 2, :, cols], tables[0], tables[1])
        held = v_ref[p // 2, :, cols]
        for c in range(CHUNKS):
            stage[c, p, 0] = turned[c * CT : (c + 1) * CT]
            stage[c, p, 1] = held[c * CT : (c + 1) * CT]
    pl.semaphore_wait(barrier, len(partners))

    def send_keys(c):
        start(key_copies(c))
        pltpu.make_async_copy(stage.at[c, y], kv.at[c, slot], yrecv.at[c]).start()

    def send_queries(c):
        start(query_copies(c))
        pltpu.make_async_copy(qst.at[y, chunk(c)], qall.at[y, chunk(c)], qrecv.at[c]).start()

    def near(c):
        arrived(group(c, 0, 0), yrecv.at[c])
        start(near_copies(c))
        sibling_copy(c, 0).start()

    def far(c):
        for n in range(2):
            arrived(group(c, 1 + n, 0), zrecv.at[c, n])
            far_copy(c, n).start()
            sibling_copy(c, 1 + n).start()

    def whole(c):
        for n in range(2):
            arrived(group(c, 3, 0, 4 * n, 4), orecv.at[c, n])
        sibling_copy(c, 3).start()

    def half(c, n):
        for r in (2 * n, 2 * n + 1):
            arrived(group(c, r, 1), brecv.at[c, r])

    send_keys(0)
    start(doc_copies())
    pltpu.make_async_copy(own_doc, docs.at[y], drecv.at[0]).start()
    send_keys(1)
    inputs[4].wait()
    for p in range(4):
        for r in range(GROUP):
            cols = pl.ds((p % 2 * GROUP + r) * HD, HD)
            qst[p, :, pl.ds(r * HD, HD)] = rotated(q_ref[p // 2, :, cols], tables[0], tables[1])
    send_queries(0)
    weights_in = [
        pltpu.make_async_copy(w_ref.at[m], wbuf.at[m], wsem.at[1 + m]) for m in range(2)
    ]
    start(weights_in)
    near(0)
    send_keys(2)
    send_queries(1)
    send_queries(2)
    send_keys(3)

    row = lax.broadcasted_iota(jnp.int32, (KEYS, HD), 0)
    col = lax.broadcasted_iota(jnp.int32, (KEYS, HD), 1)
    at = row // TILE
    rel = at // 16
    key_z = (z + jnp.where(rel == 1, 3, jnp.where(rel == 2, 1, jnp.where(rel == 3, 2, 0)))) % NZ
    key_core = (core + at // 8 % 2) % 2
    key_at = (row % TILE) * STRIPES + (at % 8 * NZ + key_z) * 2 + key_core
    kind = col - 64
    query_at = (kind % TILE) * STRIPES + index(xh, kind // TILE, z, core)
    causal[...] = jnp.where((kind >= 0) & (key_at > query_at), 1.0, 0.0).astype(jnp.bfloat16)
    vt[:, :, HD:, :] = jnp.ones((BLOCKS, 2, SUMS, HALF), jnp.bfloat16)
    qbuf[BLOCKS] = jnp.zeros((ROWS, 2 * HD), jnp.bfloat16)

    near(1)

    arrived(docs, drecv.at[0])
    seen = docs[...].astype(jnp.float32)

    def highest(values):
        return jnp.max(jnp.max(values, axis=(0, 1)).reshape(1, -1), axis=1, keepdims=True)

    cut_a = highest(seen)
    cut_b = highest(jnp.where(seen < cut_a, seen, -1.0))
    cut_c = highest(jnp.where(seen < cut_b, seen, -1.0))
    one_lane = lax.broadcasted_iota(jnp.int32, (1, HD), 1)
    cuts = jnp.where(
        one_lane == 0, cut_a, jnp.where(one_lane == 1, cut_b, jnp.where(one_lane == 2, cut_c, -5.0))
    )
    for src in range(NY):
        line = seen[src]
        dcol[src, :HD] = jnp.broadcast_to(line[:1, :HD], (HD, HD)).T
        dcol[src, HD:] = jnp.broadcast_to(line[:1, HD:], (HD, HD)).T[: TOK - HD]
    key_pos = key_at.astype(jnp.float32)

    def key_mask(j, _):
        base = (j * KEYS).astype(jnp.float32)
        kaug[j] = jnp.where(key_pos + base < cuts, 1.0, 0.0).astype(jnp.bfloat16)
        return 0

    lax.fori_loop(0, BLOCKS, key_mask, 0)

    small_lane = lax.broadcasted_iota(jnp.int32, (TILE, HD), 1)
    small_row = lax.broadcasted_iota(jnp.int32, (TILE, HD), 0)

    def take_queries(c):
        arrived(qall.at[:, chunk(c)], qrecv.at[c])

        def one(n, _):
            i = c * 2 + n
            for src in range(NY):
                hit = (dcol[src, tile(i), :] == cuts) | (small_lane == 64 + src * TILE + small_row)
                mask = jnp.where(hit, -BIG, 0.0).astype(jnp.bfloat16)
                for r in range(GROUP):
                    at = pl.ds((src * GROUP + r) * TILE, TILE)
                    qbuf[i, at, :HD] = qall[src, tile(i), pl.ds(r * HD, HD)]
                    qbuf[i, at, HD:] = mask
            return 0

        lax.fori_loop(0, 2, one, 0)

    take_queries(0)
    far(0)
    near(2)
    send_queries(3)
    send_keys(4)
    send_queries(4)
    take_queries(1)
    take_queries(2)
    half(0, 0)

    def score(buffer, i, j, n, diagonal=False):
        at = pl.ds(pl.multiple_of(n * HALF, HALF), HALF)
        slots = pl.ds(n * 32, 32)
        rows = pl.ds(pl.multiple_of(j % 2 * TILE, TILE), TILE)
        keys = kv[j // 2, slots, 0, rows, :].reshape(HALF, HD)
        mask = kaug[j, at, :]
        if diagonal:
            mask = mask + causal[at, :]
        found = lax.dot_general(
            jnp.concatenate([keys, mask], axis=1), qbuf[i], (((1,), (1,)), ((), ())),
            preferred_element_type=jnp.float32,
        )
        scores[buffer] = found
        before = highs[i, :1, :]
        now = jnp.maximum(before, jnp.max(found, axis=0, keepdims=True))
        highs[i, :1, :] = now
        tops[buffer, :1, :] = now
        tops[buffer, 1:2, :] = jnp.exp2((before - now) * SCALE)

    def absorb(buffer, i, j, n):
        top = tops[buffer, :1, :] * SCALE
        weights = jnp.exp2(scores[buffer] * SCALE - top).astype(jnp.bfloat16)
        acc[i] = acc[i] * tops[buffer, 1:2, :] + jnp.dot(
            vt[j, n], weights, preferred_element_type=jnp.float32
        )

    def finish(i):
        done = (acc[i, :HD, :] / acc[i, HD : HD + 1, :]).T.astype(jnp.bfloat16)
        for src in range(NY):
            for r in range(GROUP):
                at = (src * GROUP + r) * TILE
                ctx[src, tile(i), pl.ds(r * HD, HD)] = done[at : at + TILE]
        send_context(i)

    def turn(c, n):
        for b in range(2):
            rows = pl.ds(b * TILE, TILE)
            vt[c * 2 + b, n, :HD, :] = kv[c, pl.ds(n * 32, 32), 1, rows, :].reshape(HALF, HD).T

    services = {
        (0, 1): [(take_queries, 3), (near, 3)],
        (0, 2): [(take_queries, 4), (far, 1)],
        (0, 3): [(whole, 0), (half, 0, 1)],
        (1, 0): [(near, 4)],
        (1, 1): [(far, 2)],
        (1, 2): [(whole, 1)],
        (1, 3): [(half, 1, 0)],
        (2, 1): [(far, 3)],
        (2, 2): [(half, 1, 1)],
        (3, 0): [(whole, 2)],
        (3, 2): [(half, 2, 0)],
        (4, 1): [(far, 4), (half, 2, 1)],
        (5, 0): [(whole, 3)],
        (5, 1): [(half, 3, 0)],
        (6, 0): [(half, 3, 1)],
        (7, 0): [(whole, 4), (half, 4, 0)],
    }

    def serve(t, it):
        for (tt, nn), work in services.items():

            @pl.when((t == tt) & (it == nn))
            def _(work=work):
                for act, *args in work:
                    act(*args)

    acc[...] = jnp.zeros_like(acc)
    highs[...] = jnp.full_like(highs, LOW)
    score(4, 0, 0, 0, True)
    score(0, 1, 0, 0)
    score(1, 1, 1, 0, True)

    def body(t, _):
        c, n = t // 2, t % 2
        even, odd = c * 2, c * 2 + 1
        next_even, next_n = (t + 1) // 2 * 2, (t + 1) % 2
        turn(c, n)
        score(2, even + 2, even, n)
        absorb(4, even, even, n)

        def rest(it, _):
            i = odd + it * 2
            serve(t, it)

            def four(after):
                score(3, i + 1, odd, n)
                absorb(0, i, even, n)
                after[0]()
                absorb(1, i, odd, n)
                after[1]()
                absorb(2, i + 1, even, n)
                after[2]()
                absorb(3, i + 1, odd, n)

            @pl.when(it < 3 - c)
            def _():
                four(
                    [
                        lambda: score(0, i + 2, even, n),
                        lambda: score(1, i + 2, odd, n),
                        lambda: score(2, i + 3, even, n),
                    ]
                )

            @pl.when(it == 3 - c)
            def _():
                four(
                    [
                        lambda: score(4, next_even, next_even, next_n, True),
                        lambda: score(0, next_even + 1, next_even, next_n),
                        lambda: score(1, next_even + 1, next_even + 1, next_n, True),
                    ]
                )

            @pl.when((it == 0) & (n == 1))
            def _():
                finish(even)
                finish(odd)

            return 0

        lax.fori_loop(0, 4 - c, rest, 0)
        return 0

    lax.fori_loop(0, 8, body, 0)
    turn(4, 0)
    half(4, 1)
    turn(4, 1)
    score(2, 8, 8, 1, True)
    absorb(4, 8, 8, 0)
    score(3, 9, 8, 1)
    absorb(0, 9, 8, 0)
    score(4, 9, 9, 1, True)
    absorb(1, 9, 9, 0)
    absorb(2, 8, 8, 1)
    finish(8)
    absorb(3, 9, 8, 1)
    absorb(4, 9, 9, 1)
    finish(9)

    for copy in weights_in:
        copy.wait()

    def project(first, size, part):
        for n in range(8):
            arrived(cbuf.at[n, pl.ds(first, size)], crecv.at[n, part])

        def one(n, _):
            m = n // 4
            cols = pl.ds(pl.multiple_of(n % 4 * 512, 512), 512)
            rows = jnp.concatenate(
                [cbuf[h * 4 + m * 2 + g, first : first + size] for h in range(2) for g in range(2)],
                axis=1,
            )
            out_ref[m, first : first + size, cols] = jnp.dot(
                rows, wbuf[m, :, cols], preferred_element_type=jnp.float32
            ).astype(jnp.bfloat16)
            return 0

        lax.fori_loop(0, 8, one, 0)

    project(0, EARLY, 0)
    project(EARLY, TOK - EARLY, 1)

    for copy in doc_copies():
        copy.wait_send()

    def drain(c, _):
        for copy in (
            key_copies(c) + query_copies(c) + near_copies(c) + [far_copy(c, 0), far_copy(c, 1)]
            + [sibling_copy(c, r) for r in range(4)]
            + context_copies(c * 2) + context_copies(c * 2 + 1)
        ):
            copy.wait_send()
        return 0

    lax.fori_loop(0, CHUNKS, drain, 0)


def local(queries, keys, values, doc_start, out_weight):
    freq = np.power(500000.0, -np.arange(HD // 2) * 2.0 / HD).astype(np.float32)
    freq = jnp.asarray(np.concatenate([freq, freq])[None, :])
    width = out_weight.shape[2]
    vmem = pl.BlockSpec(memory_space=pltpu.VMEM)
    hbm = pl.BlockSpec(memory_space=pltpu.HBM)
    dma = pltpu.SemaphoreType.DMA
    b16, f32 = jnp.bfloat16, jnp.float32
    return pl.pallas_call(
        kernel,
        out_shape=jax.ShapeDtypeStruct((2, TOK, width), b16),
        in_specs=[hbm] * 6,
        out_specs=vmem,
        scratch_shapes=[
            pltpu.VMEM(freq.shape, f32),
            pltpu.VMEM(doc_start.shape, jnp.int32),
            pltpu.VMEM(queries.shape, b16),
            pltpu.VMEM(keys.shape, b16),
            pltpu.VMEM(values.shape, b16),
            pltpu.VMEM((8, 256), jnp.int32),
            pltpu.VMEM((CHUNKS, STRIPES, 2, CT, HD), b16),
            pltpu.VMEM((CHUNKS, 4, 2, CT, HD), b16),
            pltpu.VMEM((4, TOK, WIDE), b16),
            pltpu.VMEM((4, TOK, WIDE), b16),
            pltpu.VMEM((4, 8, 256), jnp.int32),
            pltpu.VMEM((2, TOK, HD), f32),
            pltpu.VMEM((4, TOK, HD), f32),
            pltpu.VMEM((BLOCKS, KEYS, HD), b16),
            pltpu.VMEM((KEYS, HD), b16),
            pltpu.VMEM((BLOCKS + 1, ROWS, 2 * HD), b16),
            pltpu.VMEM((BLOCKS, 2, HD + SUMS, HALF), b16),
            pltpu.VMEM((BUFFERS, HALF, ROWS), f32),
            pltpu.VMEM((BUFFERS, 8, ROWS), f32),
            pltpu.VMEM((BLOCKS + 1, 8, ROWS), f32),
            pltpu.VMEM((BLOCKS, HD + SUMS, ROWS), f32),
            pltpu.VMEM((4, TOK, WIDE), b16),
            pltpu.VMEM((8, TOK, WIDE), b16),
            pltpu.VMEM((2, 2048, width), b16),
            dma((CHUNKS, 7)),
            dma((CHUNKS,)),
            dma((CHUNKS, 3)),
            dma((CHUNKS,)),
            dma((3,)),
            dma((1,)),
            dma((CHUNKS, 2)),
            dma((CHUNKS, 2)),
            dma((CHUNKS, 2)),
            dma((CHUNKS, 2)),
            dma((CHUNKS, 4)),
            dma((CHUNKS, 4)),
            dma((BLOCKS, 7)),
            dma((8, 2)),
            dma((3,)),
            dma((5,)),
        ],
        compiler_params=pltpu.CompilerParams(
            collective_id=0, has_side_effects=True, vmem_limit_bytes=44 * 2**20
        ),
    )(*(pltpu.with_memory_space_constraint(x, pltpu.HBM) for x in (freq, doc_start, queries, keys, values, out_weight)))


def solution(mesh):
    return jax.shard_map(
        local,
        mesh=mesh,
        in_specs=(
            P(None, "ctx", "head"),
            P(None, "ctx", "head"),
            P(None, "ctx", "head"),
            P("ctx"),
            P(None, None, "head"),
        ),
        out_specs=P(None, "ctx", "head"),
        check_vma=False,
    )
```

time: 79.8 us -> 62.6 us (0.78)
  Pallas kernels: 75.8 us -> 61.4 us
  local copies, waits for them, and re-layouts: 3.8 us -> 1.06 us
    pallas_call x1, Pallas kernels: 75.8 us -> 61.4 us  [local(): pl.pallas_call(kernel, out_shape=jax.ShapeDtypeStruct((2, TOK, width), b1...]
    unnamed x1, local copies, waits for them, and re-layouts: 2.52 us -> 1.06 us
where the time goes in v3:
time: 62.6 us; the launch traced here: 62.5 us
  Pallas kernels  61.4 us (98%)
  local copies, waits for them, and re-layouts  1.06 us (2%)
    pallas_call x1, Pallas kernels, local(): pl.pallas_call(kernel, out_shape=jax.ShapeDtypeStruct((2, TOK, width), b1...  61.4 us

profile of v3, /device:TPU:1, one launch (start us, length us, event | category | flops | bytes accessed | tf_op | source)
XLA Modules:
  0.0 62.5 jit_solution(5843316240858407264)
XLA Ops:
  0.0 61.4 %shard_map.64 = bf16[2,160,2048]{2,1,0:T(8,128)(2,1)S(1)} custom-call(f32[1,128]{1,0:T(1,128)} %constant.2.clone.freq_hbm, s32[160]{0:T(256)} %doc_hbm.1, bf16[2,160,1024]{2,1,0:T(8,128)(2,1)} %q_hbm.1, bf16[2,160,256]{2,1,0:T(8,128)(2,1)} %k_hbm.1, bf16[2,160,256]{2,1,0:T(8,128)(2,1)} %v_hbm.1, bf16[2,2048,2048]{2,1,0:T(8,128)(2,1)} %w_ref.1), custom_call_target="tpu_custom_call" | custom-call | tf_op jit(solution)/shard_map/pallas_call | solution.py:485
  61.4 1.1 %copy.8 = bf16[2,160,2048]{2,1,0:T(8,128)(2,1)} copy(bf16[2,160,2048]{2,1,0:T(8,128)(2,1)S(1)} %shard_map.64) | data formatting | bytes 2621440

commit v4 on v3

--- a/solution.py
+++ b/solution.py
@@ -187,14 +187,14 @@
 
     def near(c):
         arrived(group(c, 0, 0), yrecv.at[c])
+        sibling_copy(c, 0).start()
         start(near_copies(c))
-        sibling_copy(c, 0).start()
 
     def far(c):
         for n in range(2):
             arrived(group(c, 1 + n, 0), zrecv.at[c, n])
+            sibling_copy(c, 1 + n).start()
             far_copy(c, n).start()
-            sibling_copy(c, 1 + n).start()
 
     def whole(c):
         for n in range(2):
@@ -350,7 +350,7 @@
         (5, 0): [(whole, 3)],
         (5, 1): [(half, 3, 0)],
         (6, 0): [(half, 3, 1)],
-        (7, 0): [(whole, 4), (half, 4, 0)],
+        (7, 0): [(half, 4, 0)],
     }
 
     def serve(t, it):
@@ -420,15 +420,16 @@
         return 0
 
     lax.fori_loop(0, 8, body, 0)
+    whole(4)
     turn(4, 0)
+    absorb(4, 8, 8, 0)
+    absorb(0, 9, 8, 0)
+    absorb(1, 9, 9, 0)
     half(4, 1)
     turn(4, 1)
     score(2, 8, 8, 1, True)
-    absorb(4, 8, 8, 0)
     score(3, 9, 8, 1)
-    absorb(0, 9, 8, 0)
     score(4, 9, 9, 1, True)
-    absorb(1, 9, 9, 0)
     absorb(2, 8, 8, 1)
     finish(8)
     absorb(3, 9, 8, 1)

time: 62.6 us -> 62 us (level)
  no operation moved by 1% of the time
where the time goes in v4:
time: 62 us; the launch traced here: 61.9 us
  Pallas kernels  60.8 us (98%)
  local copies, waits for them, and re-layouts  1.06 us (2%)
    pallas_call x1, Pallas kernels, local(): pl.pallas_call(kernel, out_shape=jax.ShapeDtypeStruct((2, TOK, width), b1...  60.8 us

profile of v4, /device:TPU:1, one launch (start us, length us, event | category | flops | bytes accessed | tf_op | source)
XLA Modules:
  0.0 61.9 jit_solution(5330911097378100823)
XLA Ops:
  0.0 60.8 %shard_map.64 = bf16[2,160,2048]{2,1,0:T(8,128)(2,1)S(1)} custom-call(f32[1,128]{1,0:T(1,128)} %constant.2.clone.freq_hbm, s32[160]{0:T(256)} %doc_hbm.1, bf16[2,160,1024]{2,1,0:T(8,128)(2,1)} %q_hbm.1, bf16[2,160,256]{2,1,0:T(8,128)(2,1)} %k_hbm.1, bf16[2,160,256]{2,1,0:T(8,128)(2,1)} %v_hbm.1, bf16[2,2048,2048]{2,1,0:T(8,128)(2,1)} %w_ref.1), custom_call_target="tpu_custom_call" | custom-call | tf_op jit(solution)/shard_map/pallas_call | solution.py:486
  60.8 1.1 %copy.8 = bf16[2,160,2048]{2,1,0:T(8,128)(2,1)} copy(bf16[2,160,2048]{2,1,0:T(8,128)(2,1)S(1)} %shard_map.64) | data formatting | bytes 2621440

commit v5 on v4

--- a/solution.py
+++ b/solution.py
@@ -444,8 +444,8 @@
             arrived(cbuf.at[n, pl.ds(first, size)], crecv.at[n, part])
 
         def one(n, _):
-            m = n // 4
-            cols = pl.ds(pl.multiple_of(n % 4 * 512, 512), 512)
+            m = n // 2
+            cols = pl.ds(pl.multiple_of(n % 2 * 1024, 1024), 1024)
             rows = jnp.concatenate(
                 [cbuf[h * 4 + m * 2 + g, first : first + size] for h in range(2) for g in range(2)],
                 axis=1,
@@ -455,7 +455,7 @@
             ).astype(jnp.bfloat16)
             return 0
 
-        lax.fori_loop(0, 8, one, 0)
+        lax.fori_loop(0, 4, one, 0)
 
     project(0, EARLY, 0)
     project(EARLY, TOK - EARLY, 1)

time: 62 us -> 60.8 us (0.981)
  Pallas kernels: 60.8 us -> 59.6 us
    pallas_call x1, Pallas kernels: 60.8 us -> 59.6 us  [local(): pl.pallas_call(kernel, out_shape=jax.ShapeDtypeStruct((2, TOK, width), b1...]
where the time goes in v5:
time: 60.8 us; the launch traced here: 60.7 us
  Pallas kernels  59.6 us (98%)
  local copies, waits for them, and re-layouts  1.06 us (2%)
    pallas_call x1, Pallas kernels, local(): pl.pallas_call(kernel, out_shape=jax.ShapeDtypeStruct((2, TOK, width), b1...  59.6 us

profile of v5, /device:TPU:1, one launch (start us, length us, event | category | flops | bytes accessed | tf_op | source)
XLA Modules:
  0.0 60.7 jit_solution(758092833550282122)
XLA Ops:
  0.0 59.6 %shard_map.64 = bf16[2,160,2048]{2,1,0:T(8,128)(2,1)S(1)} custom-call(f32[1,128]{1,0:T(1,128)} %constant.2.clone.freq_hbm, s32[160]{0:T(256)} %doc_hbm.1, bf16[2,160,1024]{2,1,0:T(8,128)(2,1)} %q_hbm.1, bf16[2,160,256]{2,1,0:T(8,128)(2,1)} %k_hbm.1, bf16[2,160,256]{2,1,0:T(8,128)(2,1)} %v_hbm.1, bf16[2,2048,2048]{2,1,0:T(8,128)(2,1)} %w_ref.1), custom_call_target="tpu_custom_call" | custom-call | tf_op jit(solution)/shard_map/pallas_call | solution.py:486
  59.6 1.1 %copy.8 = bf16[2,160,2048]{2,1,0:T(8,128)(2,1)} copy(bf16[2,160,2048]{2,1,0:T(8,128)(2,1)S(1)} %shard_map.64) | data formatting | bytes 2621440
